TPU v7x, 32 devices: a whole 2x2x4 slice. The times are simulated.
32 devices in a mesh: fsdp: 32 (over z, y, x, core).
Axes of the slice: x: 2, y: 2, z: 4, core: 2. Of those that a mesh axis runs over, the one named last changes fastest.
Arguments:
- tokens: bfloat16 [16384, 960], P('fsdp'), may hold values from -6 to 6
- attn_weight: bfloat16 [960, 2560], P(None, 'fsdp')
- ffn_weight: bfloat16 [3, 960, 2560], P(None, None, 'fsdp'), may hold values from -0.1875 to 0.1875
- norm_gains: float32 [2, 960], replicated, may hold values from 0.1 to 1.9
- seq_lengths: int32 [8], replicated, may hold values from 1024 to 4096, as said below
- cotangent: bfloat16 [16384, 960], P('fsdp'), may hold values from -6 to 6
Outputs:
- activations: bfloat16 [16384, 960], P('fsdp')
- input_grad: float32 [16384, 960], P('fsdp')
- attn_grad: float32 [960, 2560], P(None, 'fsdp')
- ffn_grad: float32 [3, 960, 2560], P(None, None, 'fsdp')
- gain_grad: float32 [2, 960], replicated
Inputs may be any that keep to these rules, and one draw needn't show every extreme that they name: `seq_lengths`: 8 lengths summing to 16384; sequences lie end to end in token order; the longest is exactly 4096 and the shortest exactly 1024.
All inputs are finite; a program needn't handle non-finite values.
Results may differ from a plain program's by a relative error of at most 0.017.
The roundings to bfloat16 on the way count: a program that leaves them out, or rounds other values in their place, can miss the bound.
Values may be sent and summed in bfloat16 or wider, within the bound.
A program may use at most 384 MiB of HBM per device.

v0:
```python
import jax
import jax.numpy as jnp
from jax import lax
from jax.sharding import PartitionSpec as P

QH = 15
KVH = 5
HD = 64
MAXLEN = 4096


EPSILON = 1e-05


def from_behind(value, axis, steps):
    count = lax.axis_size(axis)
    leading, last = (max(0, -steps), min(count, count - steps))
    return lax.ppermute(value, axis, [(source, source + steps) for source in range(leading, last)])


def for_sending(shard):

    def short(part):
        return part.astype(jnp.bfloat16) if part.dtype == jnp.float32 else part

    return jax.tree.map(short, shard)


def rms_norm(values, gain):
    factor = lax.rsqrt(jnp.mean(values * values, axis=-1, keepdims=True) + EPSILON)
    return values * factor * gain


def rotate(values, cosine, sine):
    middle = values.shape[-1] // 2
    turned = jnp.concatenate([-values[..., middle:], values[..., :middle]], axis=-1)
    return values * cosine[:, None, :] + turned * sine[:, None, :]


def unrotate(grads, cosine, sine):
    middle = grads.shape[-1] // 2
    turned = grads * sine[:, None, :]
    back_turned = jnp.concatenate([turned[..., middle:], -turned[..., :middle]], axis=-1)
    return grads * cosine[:, None, :] + back_turned


def locate(seq_lengths, places):
    ends = jnp.cumsum(seq_lengths)
    starts = ends - seq_lengths
    segment = jnp.sum((ends[None, :] <= places[:, None]).astype(jnp.int32), axis=1)
    chosen = segment[:, None] == jnp.arange(seq_lengths.shape[0], dtype=jnp.int32)[None, :]
    inside = places - jnp.sum(jnp.where(chosen, starts[None, :], 0), axis=1)
    segment = jnp.where(places < 0, -1, segment)
    return (segment, inside)


def angles(inside, head_size):
    frequency = 10000.0 ** (-2.0 * jnp.arange(head_size // 2, dtype=jnp.float32) / head_size)
    phase_angle = inside.astype(jnp.float32)[:, None] * frequency[None, :]
    cosine = jnp.cos(phase_angle)
    sine = jnp.sin(phase_angle)
    return (jnp.concatenate([cosine, cosine], axis=1), jnp.concatenate([sine, sine], axis=1))


def tokens_product(left, right):
    return lax.dot_general(
        left, right, (((0,), (0,)), ((), ())), preferred_element_type=jnp.float32
    )


def on_device(tokens, attn_weight, ffn_weight, norm_gains, seq_lengths, cotangent):
    tok_rows = tokens.shape[0]
    q_width = QH * HD
    kv_width = KVH * HD
    both = q_width + 2 * kv_width
    q_group = QH // KVH
    hop_count = (tok_rows + MAXLEN - 2) // tok_rows
    score_scale = HD ** (-0.5)
    offset = lax.axis_index("fsdp") * tok_rows
    places = offset + jnp.arange(tok_rows, dtype=jnp.int32)
    segment, inside = locate(seq_lengths, places)
    cosine, sine = angles(inside, HD)
    key_meta = []
    for step_hop in range(hop_count + 1):
        k_places = places - step_hop * tok_rows
        k_segment, k_inside = locate(seq_lengths, k_places)
        key_meta.append((k_segment, k_places))

    def hop_scores(q_heads, k_head, step_hop):
        raw = jnp.einsum("gtd,sd->gts", q_heads, k_head, preferred_element_type=jnp.float32)
        k_segment, k_places = key_meta[step_hop]
        allowed = (segment[:, None] == k_segment[None, :]) & (k_places[None, :] <= places[:, None])
        return jnp.where(allowed[None], raw * score_scale, -1e30)

    attn_full, ffn_full = (
        lax.all_gather(attn_weight, "fsdp", axis=1, tiled=True),
        lax.all_gather(ffn_weight, "fsdp", axis=2, tiled=True),
    )
    inputs = tokens.astype(jnp.float32)
    normed = rms_norm(inputs, norm_gains[0]).astype(jnp.bfloat16)
    projected = jnp.dot(normed, attn_full[:, :both], preferred_element_type=jnp.float32)
    q_raw = projected[:, :q_width].reshape(tok_rows, QH, HD)
    k_raw = projected[:, q_width : q_width + kv_width].reshape(tok_rows, KVH, HD)
    q_rot = rotate(q_raw, cosine, sine).astype(jnp.bfloat16)
    k_rot = rotate(k_raw, cosine, sine).astype(jnp.bfloat16)
    v_low = projected[:, q_width + kv_width :].astype(jnp.bfloat16)
    own_block = jnp.concatenate([k_rot.reshape(tok_rows, kv_width), v_low], axis=1)
    kv_blocks = [own_block]
    for step_hop in range(1, hop_count + 1):
        kv_blocks.append(from_behind(own_block, "fsdp", step_hop))
    kv_stack = jnp.stack(kv_blocks)
    keys_all = (
        kv_stack[:, :, :kv_width].reshape(hop_count + 1, tok_rows, KVH, HD).transpose(2, 0, 1, 3)
    )
    values_all = (
        kv_stack[:, :, kv_width:].reshape(hop_count + 1, tok_rows, KVH, HD).transpose(2, 0, 1, 3)
    )
    q_heads_all = q_rot.reshape(tok_rows, KVH, q_group, HD).transpose(1, 2, 0, 3)

    def head_forward(operands):
        q_heads, k_hops, v_hops = operands
        running_top = jnp.full((q_group, tok_rows), -1e30, jnp.float32)
        running_sum = jnp.zeros((q_group, tok_rows), jnp.float32)
        for step_hop in range(hop_count + 1):
            scores = hop_scores(q_heads, k_hops[step_hop], step_hop)
            new_top = jnp.maximum(running_top, jnp.max(scores, axis=-1))
            running_sum = running_sum * jnp.exp(running_top - new_top) + jnp.sum(
                jnp.exp(scores - new_top[..., None]), axis=-1
            )
            running_top = new_top
        log_total = running_top + jnp.log(running_sum)
        weighted = jnp.zeros((q_group, tok_rows, HD), jnp.float32)
        for step_hop in range(hop_count + 1):
            scores = hop_scores(q_heads, k_hops[step_hop], step_hop)
            probs = jnp.exp(scores - log_total[..., None]).astype(jnp.bfloat16)
            weighted = weighted + jnp.einsum(
                "gts,sd->gtd", probs, v_hops[step_hop], preferred_element_type=jnp.float32
            )
        return (weighted, log_total)

    attended, log_totals = lax.map(head_forward, (q_heads_all, keys_all, values_all))
    mixed = attended.transpose(2, 0, 1, 3).reshape(tok_rows, q_width).astype(jnp.bfloat16)
    out_cols = attn_full[:, both:]
    branch = lax.dot_general(
        mixed, out_cols, (((1,), (1,)), ((), ())), preferred_element_type=jnp.float32
    )
    middle = inputs + branch
    normed_two = rms_norm(middle, norm_gains[1]).astype(jnp.bfloat16)
    gate = jnp.dot(normed_two, ffn_full[0], preferred_element_type=jnp.float32)
    up_proj = jnp.dot(normed_two, ffn_full[1], preferred_element_type=jnp.float32)
    hidden = (jax.nn.silu(gate) * up_proj).astype(jnp.bfloat16)
    second = lax.dot_general(
        hidden, ffn_full[2], (((1,), (1,)), ((), ())), preferred_element_type=jnp.float32
    )
    activations = (middle + second).astype(jnp.bfloat16)
    attn_back, ffn_back = (
        lax.all_gather(attn_weight, "fsdp", axis=1, tiled=True),
        lax.all_gather(ffn_weight, "fsdp", axis=2, tiled=True),
    )
    d_output = cotangent.astype(jnp.float32)
    d_hidden = jnp.dot(cotangent, ffn_back[2], preferred_element_type=jnp.float32)
    _, swiglu_back = jax.vjp(lambda gate_in, up_in: jax.nn.silu(gate_in) * up_in, gate, up_proj)
    d_gate, d_up = swiglu_back(d_hidden)
    d_gate = d_gate.astype(jnp.bfloat16)
    d_up = d_up.astype(jnp.bfloat16)
    d_normed_two = lax.dot_general(
        d_gate, ffn_back[0], (((1,), (1,)), ((), ())), preferred_element_type=jnp.float32
    )
    d_normed_two = d_normed_two + lax.dot_general(
        d_up, ffn_back[1], (((1,), (1,)), ((), ())), preferred_element_type=jnp.float32
    )
    ffn_grad = None
    _, norm_two_back = jax.vjp(rms_norm, middle, norm_gains[1])
    d_mid_norm, d_gain_two = norm_two_back(d_normed_two)
    d_middle = d_output + d_mid_norm
    d_branch = d_middle.astype(jnp.bfloat16)
    d_mixed = jnp.dot(d_branch, attn_back[:, both:], preferred_element_type=jnp.float32).astype(
        jnp.bfloat16
    )
    grad_out = tokens_product(d_branch, mixed)
    d_heads_all = d_mixed.reshape(tok_rows, KVH, q_group, HD).transpose(1, 2, 0, 3)

    def head_backward(operands):
        q_heads, k_hops, v_hops, d_heads, log_total = operands
        inner = jnp.zeros((q_group, tok_rows), jnp.float32)
        for step_hop in range(hop_count + 1):
            scores = hop_scores(q_heads, k_hops[step_hop], step_hop)
            probs_full = jnp.exp(scores - log_total[..., None])
            d_probs = jnp.einsum(
                "gtd,sd->gts", d_heads, v_hops[step_hop], preferred_element_type=jnp.float32
            )
            inner = inner + jnp.sum(probs_full * d_probs, axis=-1)
        d_query = jnp.zeros((q_group, tok_rows, HD), jnp.float32)
        d_key_list = []
        d_value_list = []
        for step_hop in range(hop_count + 1):
            scores = hop_scores(q_heads, k_hops[step_hop], step_hop)
            probs_full = jnp.exp(scores - log_total[..., None])
            d_probs = jnp.einsum(
                "gtd,sd->gts", d_heads, v_hops[step_hop], preferred_element_type=jnp.float32
            )
            d_score = (probs_full * (d_probs - inner[..., None])).astype(jnp.bfloat16)
            probs = probs_full.astype(jnp.bfloat16)
            d_query = d_query + jnp.einsum(
                "gts,sd->gtd", d_score, k_hops[step_hop], preferred_element_type=jnp.float32
            )
            d_key_list.append(
                jnp.einsum("gts,gtd->sd", d_score, q_heads, preferred_element_type=jnp.float32)
            )
            d_value_list.append(
                jnp.einsum("gts,gtd->sd", probs, d_heads, preferred_element_type=jnp.float32)
            )
        return (d_query * score_scale, jnp.stack(d_key_list) * score_scale, jnp.stack(d_value_list))

    d_query_all, d_keys_all, d_values_all = lax.map(
        head_backward, (q_heads_all, keys_all, values_all, d_heads_all, log_totals)
    )
    d_key_hops = d_keys_all.transpose(1, 2, 0, 3).reshape(hop_count + 1, tok_rows, kv_width)
    d_value_hops = d_values_all.transpose(1, 2, 0, 3).reshape(hop_count + 1, tok_rows, kv_width)
    d_kv_hops = jnp.concatenate([d_key_hops, d_value_hops], axis=2)
    received = d_kv_hops[0]
    for step_hop in range(1, hop_count + 1):
        received = received + from_behind(for_sending(d_kv_hops[step_hop]), "fsdp", -step_hop)
    d_q_rot = d_query_all.transpose(2, 0, 1, 3).reshape(tok_rows, QH, HD)
    d_k_rot = received[:, :kv_width].reshape(tok_rows, KVH, HD)
    d_query_raw = unrotate(d_q_rot, cosine, sine).reshape(tok_rows, q_width)
    d_key_raw = unrotate(d_k_rot, cosine, sine).reshape(tok_rows, kv_width)
    d_projected = jnp.concatenate([d_query_raw, d_key_raw, received[:, kv_width:]], axis=1).astype(
        jnp.bfloat16
    )
    grad_proj = tokens_product(normed, d_projected)
    d_normed = lax.dot_general(
        d_projected,
        attn_back[:, :both],
        (((1,), (1,)), ((), ())),
        preferred_element_type=jnp.float32,
    )
    _, norm_one_back = jax.vjp(rms_norm, inputs, norm_gains[0])
    d_in_norm, d_gain_one = norm_one_back(d_normed)
    input_grad = d_middle + d_in_norm
    attn_terms = jnp.concatenate([grad_proj, grad_out], axis=1)
    ffn_owned = lax.psum_scatter(
        jnp.stack(
            [
                tokens_product(d_gate, normed_two),
                tokens_product(d_up, normed_two),
                tokens_product(hidden, cotangent),
            ],
            axis=1,
        ),
        "fsdp",
        scatter_dimension=0,
        tiled=True,
    )
    ffn_grad = ffn_owned.transpose(1, 2, 0)
    attn_grad = lax.psum_scatter(attn_terms, "fsdp", scatter_dimension=1, tiled=True)
    gain_grad = lax.psum(jnp.stack([d_gain_one, d_gain_two]), "fsdp")
    return (activations, input_grad, attn_grad, ffn_grad, gain_grad)


def solution(mesh):
    in_specs = (P("fsdp", None), P(None, "fsdp"), P(None, None, "fsdp"), P(), P(), P("fsdp", None))
    out_specs = (P("fsdp", None), P("fsdp", None), P(None, "fsdp"), P(None, None, "fsdp"), P())
    return jax.shard_map(
        on_device, mesh=mesh, in_specs=in_specs, out_specs=out_specs, check_vma=False
    )
```

profile of v0, /device:TPU:0, one launch (start us, length us, event | category | flops | bytes accessed | tf_op | source)
XLA Modules:
  0.0 1590.2 jit_solution(15587754417821770328)
XLA Ops:
  15.4 63.5 %all-gather.3.cloned.1.call-done = bf16[960,2560]{0,1:T(8,128)(2,1)} async-done(((bf16[960,80]{0,1:T(8,128)(2,1)}), bf16[960,2560]{0,1:T(8,128)(2,1)}) %all-gather.3.cloned.1.call-update) | async-done | bytes 4915216 | tf_op jit(solution)/shard_map/all_gather | solution.py:96
  92.1 4.7 collective-permute-start.3
  100.4 6.0 collective-permute-start.5
  107.4 29.3 %collective-permute-start.6 = (bf16[512,640]{0,1:T(8,128)(2,1)S(1)}, bf16[512,640]{0,1:T(8,128)(2,1)S(1)}, u32[]{:S(2)}, u32[]{:S(2)}) collective-permute-start(bf16[512,640]{0,1:T(8,128)(2,1)S(1)} %pad_maximum_fusion.7), channel_id=1, source_target_pairs={{0,7},{1,8},{2,9},{3,10},{4,11},{5,12},{6,13},{7,14},{8,15},{9,16}... | collective-permute-start | bytes 1966088 | tf_op jit(solution)/shard_map/ppermute | solution.py:18
  140.2 7.6 collective-permute-done.4
  155.3 294.9 %while.34 = (s32[]{:T(128)}, bf16[5,3,512,64]{2,3,1,0:T(8,128)(2,1)}, f32[5,3,512]{2,1,0:T(4,128)}, s32[512]{0:T(512)S(1)}, bf16[5,3,512,64]{2,3,1,0:T(8,128)(2,...) while((s32[]{:T(128)}, ...), condition=%wide.region_31.32_spmd.clone.clone.clone, body=%wide.region_12.31_spmd.clone.clone.sunk.clone | while | flops 1897754624 | bytes 202161424 | solution.py:141
  455.0 7.3 fusion.332
  463.9 6.1 fusion.334
  470.0 10.0 multiply_convert_fusion.9
  487.4 5.2 fusion.331
  492.6 8.2 multiply_reduce_fusion.9
  505.3 9.9 pad_maximum_fusion
  515.1 44.6 %copy.136 = f32[2560,3,960]{2,1,0:T(4,128)} copy(f32[2560,3,960]{0,2,1:T(8,128)} %pad_maximum_fusion) | data formatting | bytes 58982400 | tf_op jit(solution)/shard_map/stack | solution.py:243
  566.4 566.4 %while.35 = (s32[]{:T(128)}, f32[5,3,512,64]{2,3,1,0:T(8,128)}, f32[5,9,512,64]{2,3,1,0:T(8,128)}, f32[5,9,512,64]{2,3,1,0:T(8,128)}, s32[512]{0:T(512)S(1)}, /*...) while((s32[]{:T(128)}, f32[5,3,512,64]{2,3,1,0:T(8,128)}, ...), condition=%wide.region_44.45_spmd.clone.clone.clone, body=%wide.region_34.44_spmd.clone.clone.sunk.clone | while | flops 4601814016 | bytes 531139808 | solution.py:215
  637.6 22.9 %multiply_convert_fusion.14 = (bf16[3,512,512]{1,2,0:T(8,128)(2,1)S(1)}, bf16[3,512,512]{1,2,0:T(8,128)(2,1)}, bf16[3,512,512]{1,2,0:T(8,128)(2,1)}, bf16[3,512,...) fusion(f32[3,512,512]{1,2,0:T(8,128)} %get-tuple-element.1307, ...), kind=kLoop, calls=%fused_computation.219.clone.1.clone | loop fusion | flops 21233664 | bytes 70785024 | tf_op jit(solution)/shard_map/while/body/eval_jaxpr/convert_element_type | solution.py:202
  746.1 25.0 %multiply_convert_fusion.14 = (bf16[3,512,512]{1,2,0:T(8,128)(2,1)S(1)}, bf16[3,512,512]{1,2,0:T(8,128)(2,1)}, bf16[3,512,512]{1,2,0:T(8,128)(2,1)}, bf16[3,512,...) fusion(f32[3,512,512]{1,2,0:T(8,128)} %get-tuple-element.1307, ...), kind=kLoop, calls=%fused_computation.219.clone.1.clone | loop fusion | flops 21233664 | bytes 70785024 | tf_op jit(solution)/shard_map/while/body/eval_jaxpr/convert_element_type | solution.py:202
  857.3 24.0 %multiply_convert_fusion.14 = (bf16[3,512,512]{1,2,0:T(8,128)(2,1)S(1)}, bf16[3,512,512]{1,2,0:T(8,128)(2,1)}, bf16[3,512,512]{1,2,0:T(8,128)(2,1)}, bf16[3,512,...) fusion(f32[3,512,512]{1,2,0:T(8,128)} %get-tuple-element.1307, ...), kind=kLoop, calls=%fused_computation.219.clone.1.clone | loop fusion | flops 21233664 | bytes 70785024 | tf_op jit(solution)/shard_map/while/body/eval_jaxpr/convert_element_type | solution.py:202
  935.0 4.7 multiply_reduce_fusion.33
  967.1 23.8 %multiply_convert_fusion.14 = (bf16[3,512,512]{1,2,0:T(8,128)(2,1)S(1)}, bf16[3,512,512]{1,2,0:T(8,128)(2,1)}, bf16[3,512,512]{1,2,0:T(8,128)(2,1)}, bf16[3,512,...) fusion(f32[3,512,512]{1,2,0:T(8,128)} %get-tuple-element.1307, ...), kind=kLoop, calls=%fused_computation.219.clone.1.clone | loop fusion | flops 21233664 | bytes 70785024 | tf_op jit(solution)/shard_map/while/body/eval_jaxpr/convert_element_type | solution.py:202
  1045.5 4.7 multiply_reduce_fusion.33
  1077.6 23.7 %multiply_convert_fusion.14 = (bf16[3,512,512]{1,2,0:T(8,128)(2,1)S(1)}, bf16[3,512,512]{1,2,0:T(8,128)(2,1)}, bf16[3,512,512]{1,2,0:T(8,128)(2,1)}, bf16[3,512,...) fusion(f32[3,512,512]{1,2,0:T(8,128)} %get-tuple-element.1307, ...), kind=kLoop, calls=%fused_computation.219.clone.1.clone | loop fusion | flops 21233664 | bytes 70785024 | tf_op jit(solution)/shard_map/while/body/eval_jaxpr/convert_element_type | solution.py:202
  1132.8 6.5 copy.134
  1142.5 8.3 fusion.326
  1161.2 30.0 %collective-permute-done.15 = bf16[512,640]{0,1:T(8,128)(2,1)S(1)} collective-permute-done((bf16[512,640]{0,1:T(8,128)(2,1)S(1)}, bf16[512,640]{0,1:T(8,128)(2,1)S(1)}, u32[]{:S(2)}, u32[]{:S(2)}) %collective-permute-start.15) | collective-permute-done | bytes 655392 | tf_op jit(solution)/shard_map/ppermute | solution.py:18
  1192.5 109.3 %collective-permute-done.14 = bf16[512,640]{0,1:T(8,128)(2,1)S(1)} collective-permute-done((bf16[512,640]{0,1:T(8,128)(2,1)S(1)}, bf16[512,640]{0,1:T(8,128)(2,1)S(1)}, u32[]{:S(2)}, u32[]{:S(2)}) %collective-permute-start.14) | collective-permute-done | bytes 655392 | tf_op jit(solution)/shard_map/ppermute | solution.py:18
  1309.9 7.3 collective-permute-done.9
  1324.0 9.8 pad_maximum_fusion.2
  1333.9 11.4 copy.175
  1345.3 7.7 add_convert_fusion
  1353.1 5.4 fusion.344
  1358.5 128.4 %psum.7 = f32[2,960]{1,0:T(2,128)} all-reduce(f32[2,960]{1,0:T(2,128)S(1)} %pad_maximum_fusion.11), channel_id=1, replica_groups=mesh['fsdp'=32] {'fsdp'}, use_global_device_ids=true, to_apply=%region_50.51 | all-reduce | flops 1920 | bytes 15360 | tf_op jit(solution)/shard_map/psum | solution.py:257
  1493.3 90.2 %reduce-scatter.4.cloned.1.call-done = f32[80,960]{1,0:T(8,128)} async-done(((f32[2560,960]{1,0:T(8,128)}), f32[80,960]{1,0:T(8,128)}) %reduce-scatter.4.cloned.1.call-update) | async-done | bytes 307216
  (1276 shorter events, 808.2 us)
Async XLA Ops:
  7.2 71.7 %copy-start.48 = (bf16[512,960]{0,1:T(8,128)(2,1)S(1)}, bf16[512,960]{0,1:T(8,128)(2,1)}, u32[]{:S(2)}) copy-start(bf16[512,960]{0,1:T(8,128)(2,1)} %param.10) | copy-start | bytes 2949124
  7.2 71.7 %all-gather.3.cloned.1.call-start = ((), (), s32[]{:S(2)}) async-start(), calls=%async_computation.1 | async-start | bytes 5406720 | tf_op jit(solution)/shard_map/all_gather | solution.py:96
  7.9 445.9 %all-gather.5.cloned.1.call-start = ((), (), s32[]{:S(2)}) async-start(), calls=%async_computation.2 | async-start | bytes 16220160 | tf_op jit(solution)/shard_map/all_gather | solution.py:97
  8.7 1481.5 %all-reduce.3.cloned.1.call-start = ((), (), s32[]{:S(2)}) async-start(), calls=%async_computation.4 | async-start | bytes 83886080
  12.8 69.9 %copy-start.83 = (f32[1,960]{1,0:T(1,128)}, f32[1,960]{1,0:T(1,128)S(1)}, u32[]{:S(2)}) copy-start(f32[1,960]{1,0:T(1,128)S(1)} %get-tuple-element.808) | copy-start | bytes 11524
  14.3 68.4 %copy-start.85 = (f32[512]{0:T(512)}, f32[512]{0:T(512)S(1)}, u32[]{:S(2)}) copy-start(f32[512]{0:T(512)S(1)} %fusion.394) | copy-start | bytes 6148
  15.2 83.6 %copy-start.53 = (f32[512,64]{0,1:T(8,128)}, f32[512,64]{0,1:T(8,128)S(1)}, u32[]{:S(2)}) copy-start(f32[512,64]{0,1:T(8,128)S(1)} %pad_maximum_fusion.10) | copy-start | bytes 393220
  15.3 83.6 %copy-start.51 = (f32[512,64]{0,1:T(8,128)}, f32[512,64]{0,1:T(8,128)S(1)}, u32[]{:S(2)}) copy-start(f32[512,64]{0,1:T(8,128)S(1)} %pad_maximum_fusion.9) | copy-start | bytes 393220
  83.4 17.0 %collective-permute-start = (bf16[512,640]{0,1:T(8,128)(2,1)S(1)}, bf16[512,640]{0,1:T(8,128)(2,1)S(1)}, u32[]{:S(2)}, u32[]{:S(2)}) collective-permute-start(bf16[512,640]{0,1:T(8,128)(2,1)S(1)} %pad_maximum_fusion.7), channel_id=1, source_target_pairs={{0,1},{1,2},{2,3},{3,4},{4,5},{5,6},{6,7},{7,8},{8,9},{9,10},{10,1... | collective-permute-start | bytes 1966088 | tf_op jit(solution)/shard_map/ppermute | solution.py:18
  85.6 21.8 %collective-permute-start.1 = (bf16[512,640]{0,1:T(8,128)(2,1)S(1)}, bf16[512,640]{0,1:T(8,128)(2,1)S(1)}, u32[]{:S(2)}, u32[]{:S(2)}) collective-permute-start(bf16[512,640]{0,1:T(8,128)(2,1)S(1)} %pad_maximum_fusion.7), channel_id=1, source_target_pairs={{0,2},{1,3},{2,4},{3,5},{4,6},{5,7},{6,8},{7,9},{8,10},{9,11},{10,... | collective-permute-start | bytes 1966088 | tf_op jit(solution)/shard_map/ppermute | solution.py:18
  89.0 47.9 %collective-permute-start.2 = (bf16[512,640]{0,1:T(8,128)(2,1)S(1)}, bf16[512,640]{0,1:T(8,128)(2,1)S(1)}, u32[]{:S(2)}, u32[]{:S(2)}) collective-permute-start(bf16[512,640]{0,1:T(8,128)(2,1)S(1)} %pad_maximum_fusion.7), channel_id=1, source_target_pairs={{0,3},{1,4},{2,5},{3,6},{4,7},{5,8},{6,9},{7,10},{8,11},{9,12},{10... | collective-permute-start | bytes 1966088 | tf_op jit(solution)/shard_map/ppermute | solution.py:18
  92.1 48.0 %collective-permute-start.3 = (bf16[512,640]{0,1:T(8,128)(2,1)S(1)}, bf16[512,640]{0,1:T(8,128)(2,1)S(1)}, u32[]{:S(2)}, u32[]{:S(2)}) collective-permute-start(bf16[512,640]{0,1:T(8,128)(2,1)S(1)} %pad_maximum_fusion.7), channel_id=1, source_target_pairs={{0,4},{1,5},{2,6},{3,7},{4,8},{5,9},{6,10},{7,11},{8,12},{9,13},{1... | collective-permute-start | bytes 1966088 | tf_op jit(solution)/shard_map/ppermute | solution.py:18
  96.8 51.0 %collective-permute-start.4 = (bf16[512,640]{0,1:T(8,128)(2,1)S(1)}, bf16[512,640]{0,1:T(8,128)(2,1)S(1)}, u32[]{:S(2)}, u32[]{:S(2)}) collective-permute-start(bf16[512,640]{0,1:T(8,128)(2,1)S(1)} %pad_maximum_fusion.7), channel_id=1, source_target_pairs={{0,5},{1,6},{2,7},{3,8},{4,9},{5,10},{6,11},{7,12},{8,13},{9,14},{... | collective-permute-start | bytes 1966088 | tf_op jit(solution)/shard_map/ppermute | solution.py:18
  100.4 47.5 %collective-permute-start.5 = (bf16[512,640]{0,1:T(8,128)(2,1)S(1)}, bf16[512,640]{0,1:T(8,128)(2,1)S(1)}, u32[]{:S(2)}, u32[]{:S(2)}) collective-permute-start(bf16[512,640]{0,1:T(8,128)(2,1)S(1)} %pad_maximum_fusion.7), channel_id=1, source_target_pairs={{0,6},{1,7},{2,8},{3,9},{4,10},{5,11},{6,12},{7,13},{8,14},{9,15},... | collective-permute-start | bytes 1966088 | tf_op jit(solution)/shard_map/ppermute | solution.py:18
  107.4 40.5 %collective-permute-start.6 = (bf16[512,640]{0,1:T(8,128)(2,1)S(1)}, bf16[512,640]{0,1:T(8,128)(2,1)S(1)}, u32[]{:S(2)}, u32[]{:S(2)}) collective-permute-start(bf16[512,640]{0,1:T(8,128)(2,1)S(1)} %pad_maximum_fusion.7), channel_id=1, source_target_pairs={{0,7},{1,8},{2,9},{3,10},{4,11},{5,12},{6,13},{7,14},{8,15},{9,16}... | collective-permute-start | bytes 1966088 | tf_op jit(solution)/shard_map/ppermute | solution.py:18
  136.8 13.8 collective-permute-start.7
  453.5 106.3 %copy-start.47 = (f32[512,960]{0,1:T(8,128)}, f32[512,960]{0,1:T(8,128)S(1)}, u32[]{:S(2)}) copy-start(f32[512,960]{0,1:T(8,128)S(1)} %get-tuple-element.812) | copy-start | bytes 5898244
  559.8 1023.7 %reduce-scatter.4.cloned.1.call-start = ((), (), s32[]{:S(2)}) async-start(), calls=%async_computation.3 | async-start | bytes 10813440
  1154.4 36.8 %collective-permute-start.15 = (bf16[512,640]{0,1:T(8,128)(2,1)S(1)}, bf16[512,640]{0,1:T(8,128)(2,1)S(1)}, u32[]{:S(2)}, u32[]{:S(2)}) collective-permute-start(bf16[512,640]{0,1:T(8,128)(2,1)S(1)} %get-tuple-element.790), channel_id=1, source_target_pairs={{8,0},{9,1},{10,2},{11,3},{12,4},{13,5},{14,6},{15,7},{16,8},{17,9... | collective-permute-start | bytes 1966088 | tf_op jit(solution)/shard_map/ppermute | solution.py:18
  1155.7 146.1 %collective-permute-start.14 = (bf16[512,640]{0,1:T(8,128)(2,1)S(1)}, bf16[512,640]{0,1:T(8,128)(2,1)S(1)}, u32[]{:S(2)}, u32[]{:S(2)}) collective-permute-start(bf16[512,640]{0,1:T(8,128)(2,1)S(1)} %get-tuple-element.791), channel_id=1, source_target_pairs={{7,0},{8,1},{9,2},{10,3},{11,4},{12,5},{13,6},{14,7},{15,8},{16,9}... | collective-permute-start | bytes 1966088 | tf_op jit(solution)/shard_map/ppermute | solution.py:18
  1157.0 146.1 %collective-permute-start.13 = (bf16[512,640]{0,1:T(8,128)(2,1)S(1)}, bf16[512,640]{0,1:T(8,128)(2,1)S(1)}, u32[]{:S(2)}, u32[]{:S(2)}) collective-permute-start(bf16[512,640]{0,1:T(8,128)(2,1)S(1)} %get-tuple-element.792), channel_id=1, source_target_pairs={{6,0},{7,1},{8,2},{9,3},{10,4},{11,5},{12,6},{13,7},{14,8},{15,9},... | collective-permute-start | bytes 1966088 | tf_op jit(solution)/shard_map/ppermute | solution.py:18
  1158.3 151.6 %collective-permute-start.12 = (bf16[512,640]{0,1:T(8,128)(2,1)S(1)}, bf16[512,640]{0,1:T(8,128)(2,1)S(1)}, u32[]{:S(2)}, u32[]{:S(2)}) collective-permute-start(bf16[512,640]{0,1:T(8,128)(2,1)S(1)} %get-tuple-element.793), channel_id=1, source_target_pairs={{5,0},{6,1},{7,2},{8,3},{9,4},{10,5},{11,6},{12,7},{13,8},{14,9},{... | collective-permute-start | bytes 1966088 | tf_op jit(solution)/shard_map/ppermute | solution.py:18
  1159.6 150.3 %collective-permute-start.11 = (bf16[512,640]{0,1:T(8,128)(2,1)S(1)}, bf16[512,640]{0,1:T(8,128)(2,1)S(1)}, u32[]{:S(2)}, u32[]{:S(2)}) collective-permute-start(bf16[512,640]{0,1:T(8,128)(2,1)S(1)} %get-tuple-element.794), channel_id=1, source_target_pairs={{4,0},{5,1},{6,2},{7,3},{8,4},{9,5},{10,6},{11,7},{12,8},{13,9},{1... | collective-permute-start | bytes 1966088 | tf_op jit(solution)/shard_map/ppermute | solution.py:18
  1191.2 118.7 %collective-permute-start.10 = (bf16[512,640]{0,1:T(8,128)(2,1)S(1)}, bf16[512,640]{0,1:T(8,128)(2,1)S(1)}, u32[]{:S(2)}, u32[]{:S(2)}) collective-permute-start(bf16[512,640]{0,1:T(8,128)(2,1)S(1)} %get-tuple-element.795), channel_id=1, source_target_pairs={{3,0},{4,1},{5,2},{6,3},{7,4},{8,5},{9,6},{10,7},{11,8},{12,9},{13... | collective-permute-start | bytes 1966088 | tf_op jit(solution)/shard_map/ppermute | solution.py:18
  1301.8 15.4 collective-permute-start.9
  1303.1 14.1 collective-permute-start.8
  1305.0 12.2 slice-start
  1305.0 12.2 slice-start.2
  1306.6 11.9 copy-start.55
  1306.6 10.6 slice-start.1
  1306.6 10.6 slice-start.3
  1353.0 133.8 %copy-start.82 = (f32[512]{0:T(512)S(1)}, f32[512]{0:T(512)}, u32[]{:S(2)}) copy-start(f32[512]{0:T(512)} %copy-done.81) | copy-start | bytes 6148
  (332 other events, 1264.8 us)
Sparse Core Ops, SparseCore 0:
  10.9 67.9 all-gather.2
  81.7 182.8 all-gather.4
  559.9 844.0 all-reduce.2
  1406.8 176.6 reduce-scatter.3
where the time goes:
time: 1600 us; the launch traced here: 1590 us
  matrix products  685 us (43%)
  waiting for transfers between devices  313 us (20%)
  other arithmetic  238 us (15%)
  blocking collectives  128 us (8%)
  local copies, waits for them, and re-layouts  125 us (8%)
  starting transfers between devices  64.3 us (4%)
  loops' own time  21.4 us (1%)
    dot_general x90, matrix products, hop_scores(): jnp.einsum('gtd,sd->gts', q_heads, k_head, preferred_element_type=jnp.flo...  325 us
    ppermute x16, waiting for transfers between devices, from_behind(): lax.ppermute(value, axis, [(source, source + steps) for source in range(l...  158 us
    psum x1, blocking collectives, on_device(): gain_grad = lax.psum(jnp.stack([d_gain_one, d_gain_two]), 'fsdp')  128 us
    convert_element_type x5, other arithmetic, head_backward(): d_score = (probs_full * (d_probs - inner[..., None])).astype(jnp.bfloat16)  119 us
    unnamed x6, waiting for transfers between devices  91.6 us
    dot_general x45, matrix products, head_forward(): jnp.einsum('gts,sd->gtd', probs, v_hops[step_hop], preferred_element_type...  86.1 us
    dot_general x45, matrix products, head_backward(): jnp.einsum('gts,sd->gtd', d_score, k_hops[step_hop], preferred_element_ty...  69.9 us
    dot_general x45, matrix products, head_backward(): jnp.einsum('gtd,sd->gts', d_heads, v_hops[step_hop], preferred_element_ty...  69.3 us
  transfers between devices with their start and end apart: 20, of which 8 were waited for; matrix products, arithmetic and copies ran while one was open for 57% of the time, Pallas kernels for 0%

commit v1 on v0

v1 whole, which is shorter than its diff:
```python
import jax
import jax.numpy as jnp
from jax import lax
from jax.experimental import pallas as pl
from jax.experimental.pallas import tpu as pltpu
from jax.sharding import PartitionSpec as P

QH = 15
KVH = 5
HD = 64
MAXLEN = 4096
GROUP = QH // KVH
EPSILON = 1e-05
VMEM_LIMIT = 48 * 1024 * 1024


def from_behind(value, axis, steps):
    count = lax.axis_size(axis)
    leading, last = (max(0, -steps), min(count, count - steps))
    return lax.ppermute(value, axis, [(source, source + steps) for source in range(leading, last)])


def rms_norm(values, gain):
    factor = lax.rsqrt(jnp.mean(values * values, axis=-1, keepdims=True) + EPSILON)
    return values * factor * gain


def rotate(values, cosine, sine):
    first, second = (values[:, : HD // 2], values[:, HD // 2 :])
    return jnp.concatenate(
        [first * cosine - second * sine, second * cosine + first * sine], axis=1
    )


def unrotate(grads, cosine, sine):
    first, second = (grads[:, : HD // 2], grads[:, HD // 2 :])
    return jnp.concatenate(
        [first * cosine + second * sine, second * cosine - first * sine], axis=1
    )


def locate(seq_lengths, places):
    ends = jnp.cumsum(seq_lengths)
    starts = ends - seq_lengths
    segment = jnp.sum((ends[None, :] <= places[:, None]).astype(jnp.int32), axis=1)
    chosen = segment[:, None] == jnp.arange(seq_lengths.shape[0], dtype=jnp.int32)[None, :]
    return jnp.sum(jnp.where(chosen, starts[None, :], 0), axis=1)


def dot(left, right, contract):
    return lax.dot_general(
        left, right, (((contract[0],), (contract[1],)), ((), ())),
        preferred_element_type=jnp.float32,
    )


def masked(scores, info_ref, starts_ref, hop):
    rows, columns = scores.shape
    offset = info_ref[0]
    key_place = offset - hop * rows + lax.broadcasted_iota(jnp.int32, scores.shape, 0)
    query_place = offset + lax.broadcasted_iota(jnp.int32, (1, columns), 1)
    allowed = (key_place >= starts_ref[...]) & (key_place <= query_place)
    return jnp.where(allowed, scores, -1e30)


def block_kind(info_ref, hop, rows):
    key_first = info_ref[0] - hop * rows
    used = (key_first + rows > info_ref[1]) & (key_first + rows > 0)
    whole = (hop > 0) & (key_first >= info_ref[2])
    return (used & whole, used & jnp.logical_not(whole), jnp.logical_not(used))


def forward_kernel(info_ref, starts_ref, q_ref, k_ref, v_ref, o_ref, lse_ref, top, total):
    hop = pl.program_id(1)
    rows = k_ref.shape[1]

    @pl.when(hop == 0)
    def _():
        top[...] = jnp.full_like(top, -1e30)
        total[...] = jnp.zeros_like(total)
        o_ref[...] = jnp.zeros_like(o_ref)

    def work(mask):
        keys = k_ref[...].T
        for g in range(GROUP):
            head = slice(g * HD, (g + 1) * HD)
            scores = dot(keys, q_ref[head, :], (1, 0))
            if mask:
                scores = masked(scores, info_ref, starts_ref, hop)
            old = top[g : g + 1, :]
            new = jnp.maximum(old, jnp.max(scores, axis=0, keepdims=True))
            probs = jnp.exp(scores - new)
            shrink = jnp.exp(old - new)
            total[g : g + 1, :] = total[g : g + 1, :] * shrink + jnp.sum(
                probs, axis=0, keepdims=True
            )
            top[g : g + 1, :] = new
            o_ref[head, :] = o_ref[head, :] * shrink + dot(
                v_ref[...], probs.astype(jnp.bfloat16), (1, 0)
            )

    whole, part, _ = block_kind(info_ref, hop, rows)

    @pl.when(whole)
    def _():
        work(False)

    @pl.when(part)
    def _():
        work(True)

    @pl.when(hop == pl.num_programs(1) - 1)
    def _():
        for g in range(GROUP):
            head = slice(g * HD, (g + 1) * HD)
            o_ref[head, :] = o_ref[head, :] / total[g : g + 1, :]
            lse_ref[g : g + 1, :] = top[g : g + 1, :] + jnp.log(total[g : g + 1, :])


def backward_kernel(
    info_ref, starts_ref, q_ref, k_ref, v_ref, do_ref, lse_ref, inner_ref, dq_ref, dkv_ref
):
    hop = pl.program_id(1)
    rows = k_ref.shape[1]

    @pl.when(hop == 0)
    def _():
        dq_ref[...] = jnp.zeros_like(dq_ref)

    def work(mask):
        keys = k_ref[...].T
        values = v_ref[...].T
        d_keys = d_values = None
        for g in range(GROUP):
            head = slice(g * HD, (g + 1) * HD)
            scores = dot(keys, q_ref[head, :], (1, 0))
            if mask:
                scores = masked(scores, info_ref, starts_ref, hop)
            probs = jnp.exp(scores - lse_ref[g : g + 1, :])
            d_probs = dot(values, do_ref[head, :], (1, 0))
            d_scores = (probs * (d_probs - inner_ref[g : g + 1, :])).astype(jnp.bfloat16)
            d_value = dot(probs.astype(jnp.bfloat16), do_ref[head, :], (1, 1))
            d_key = dot(d_scores, q_ref[head, :], (1, 1))
            d_values = d_value if d_values is None else d_values + d_value
            d_keys = d_key if d_keys is None else d_keys + d_key
            dq_ref[head, :] += dot(k_ref[...], d_scores, (1, 0))
        dkv_ref[...] = jnp.concatenate([d_keys, d_values], axis=1).T.astype(dkv_ref.dtype)

    whole, part, unused = block_kind(info_ref, hop, rows)

    @pl.when(whole)
    def _():
        work(False)

    @pl.when(part)
    def _():
        work(True)

    @pl.when(unused)
    def _():
        dkv_ref[...] = jnp.zeros_like(dkv_ref)


def attention_specs(tok_rows):
    starts = pl.BlockSpec((1, tok_rows), lambda h, j, *_: (0, 0))
    wide = pl.BlockSpec((None, GROUP * HD, tok_rows), lambda h, j, *_: (h, 0, 0))
    key = pl.BlockSpec((None, HD, tok_rows), lambda h, j, *_: (j, h, 0))
    value = pl.BlockSpec((None, HD, tok_rows), lambda h, j, *_: (j, KVH + h, 0))
    line = pl.BlockSpec((None, GROUP, tok_rows), lambda h, j, *_: (h, 0, 0))
    return (starts, wide, key, value, line)


def attention_forward(info, starts_row, queries, kv_stack):
    hops, _, tok_rows = kv_stack.shape
    starts, wide, key, value, line = attention_specs(tok_rows)
    pairs = QH * hops * tok_rows * tok_rows
    return pl.pallas_call(
        forward_kernel,
        grid_spec=pltpu.PrefetchScalarGridSpec(
            num_scalar_prefetch=1,
            grid=(KVH, hops),
            in_specs=[starts, wide, key, value],
            out_specs=[wide, line],
            scratch_shapes=[pltpu.VMEM((8, tok_rows), jnp.float32)] * 2,
        ),
        out_shape=[
            jax.ShapeDtypeStruct((KVH, GROUP * HD, tok_rows), jnp.float32),
            jax.ShapeDtypeStruct((KVH, GROUP, tok_rows), jnp.float32),
        ],
        compiler_params=pltpu.CompilerParams(vmem_limit_bytes=VMEM_LIMIT),
        cost_estimate=pl.CostEstimate(
            flops=16 * HD * pairs, bytes_accessed=12 << 20, transcendentals=pairs
        ),
        name="attention_forward",
    )(info, starts_row, queries, kv_stack, kv_stack)


def attention_backward(info, starts_row, queries, kv_stack, d_heads, lse, inner):
    hops, _, tok_rows = kv_stack.shape
    starts, wide, key, value, line = attention_specs(tok_rows)
    pairs = QH * hops * tok_rows * tok_rows
    grads = pl.BlockSpec((None, None, 2 * HD, tok_rows), lambda h, j, *_: (j, h, 0, 0))
    return pl.pallas_call(
        backward_kernel,
        grid_spec=pltpu.PrefetchScalarGridSpec(
            num_scalar_prefetch=1,
            grid=(KVH, hops),
            in_specs=[starts, wide, key, value, wide, line, line],
            out_specs=[wide, grads],
        ),
        out_shape=[
            jax.ShapeDtypeStruct((KVH, GROUP * HD, tok_rows), jnp.float32),
            jax.ShapeDtypeStruct((hops, KVH, 2 * HD, tok_rows), jnp.bfloat16),
        ],
        compiler_params=pltpu.CompilerParams(vmem_limit_bytes=VMEM_LIMIT),
        cost_estimate=pl.CostEstimate(
            flops=40 * HD * pairs, bytes_accessed=24 << 20, transcendentals=pairs
        ),
        name="attention_backward",
    )(info, starts_row, queries, kv_stack, kv_stack, d_heads, lse, inner)


def scattered_sum(terms):
    return lax.psum_scatter(
        terms.astype(jnp.bfloat16), "fsdp", scatter_dimension=0, tiled=True
    ).astype(jnp.float32)


def on_device(tokens, attn_weight, ffn_weight, norm_gains, seq_lengths, cotangent):
    tok_rows = tokens.shape[0]
    q_width = QH * HD
    kv_width = KVH * HD
    both = q_width + 2 * kv_width
    hop_count = (tok_rows + MAXLEN - 2) // tok_rows
    score_scale = HD ** (-0.5)
    offset = lax.axis_index("fsdp") * tok_rows
    places = offset + jnp.arange(tok_rows, dtype=jnp.int32)
    starts = locate(seq_lengths, places)
    inside = places - starts
    frequency = 10000.0 ** (-2.0 * jnp.arange(HD // 2, dtype=jnp.float32) / HD)
    phase_angle = frequency[:, None] * inside.astype(jnp.float32)[None, :]
    cosine, sine = (jnp.cos(phase_angle), jnp.sin(phase_angle))
    info = jnp.stack([offset, starts[0], starts[-1]]).astype(jnp.int32)
    starts_row = starts[None, :].astype(jnp.int32)

    attn_full = lax.all_gather(attn_weight, "fsdp", axis=1, tiled=True)
    ffn_full = lax.all_gather(ffn_weight, "fsdp", axis=2, tiled=True)
    inputs = tokens.astype(jnp.float32)
    normed = rms_norm(inputs, norm_gains[0]).astype(jnp.bfloat16)
    projected = dot(attn_full[:, :both], normed, (0, 1))
    q_rot = rotate(projected[:q_width].reshape(QH, HD, tok_rows), cosine, sine)
    q_rot = q_rot.astype(jnp.bfloat16) * jnp.bfloat16(score_scale)
    k_rot = rotate(projected[q_width : q_width + kv_width].reshape(KVH, HD, tok_rows), cosine, sine)
    own_block = jnp.concatenate(
        [k_rot.reshape(kv_width, tok_rows), projected[q_width + kv_width :]], axis=0
    ).astype(jnp.bfloat16)
    kv_stack = jnp.stack(
        [own_block] + [from_behind(own_block, "fsdp", hop) for hop in range(1, hop_count + 1)]
    )
    queries = q_rot.reshape(KVH, GROUP * HD, tok_rows)
    attended, lse = attention_forward(info, starts_row, queries, kv_stack)
    mixed = attended.reshape(q_width, tok_rows).astype(jnp.bfloat16)
    out_cols = attn_full[:, both:]
    middle = inputs + dot(mixed, out_cols, (0, 1))
    normed_two = rms_norm(middle, norm_gains[1]).astype(jnp.bfloat16)
    gate = dot(normed_two, ffn_full[0], (1, 0))
    up_proj = dot(normed_two, ffn_full[1], (1, 0))
    hidden = (jax.nn.silu(gate) * up_proj).astype(jnp.bfloat16)
    activations = (middle + dot(hidden, ffn_full[2], (1, 1))).astype(jnp.bfloat16)

    d_output = cotangent.astype(jnp.float32)
    d_hidden = dot(cotangent, ffn_full[2], (1, 0))
    _, swiglu_back = jax.vjp(lambda gate_in, up_in: jax.nn.silu(gate_in) * up_in, gate, up_proj)
    d_gate, d_up = swiglu_back(d_hidden)
    d_gate = d_gate.astype(jnp.bfloat16)
    d_up = d_up.astype(jnp.bfloat16)
    ffn_owned = [
        scattered_sum(dot(hidden, cotangent, (0, 0))),
        scattered_sum(dot(d_gate, normed_two, (0, 0))),
        scattered_sum(dot(d_up, normed_two, (0, 0))),
    ]
    ffn_grad = jnp.stack([ffn_owned[1].T, ffn_owned[2].T, ffn_owned[0].T])
    d_normed_two = dot(d_gate, ffn_full[0], (1, 1)) + dot(d_up, ffn_full[1], (1, 1))
    _, norm_two_back = jax.vjp(rms_norm, middle, norm_gains[1])
    d_mid_norm, d_gain_two = norm_two_back(d_normed_two)
    d_middle = d_output + d_mid_norm
    d_branch = d_middle.astype(jnp.bfloat16)
    d_mixed = dot(out_cols, d_branch, (0, 1)).astype(jnp.bfloat16)
    grad_out = dot(mixed, d_branch, (1, 0))
    d_heads = d_mixed.reshape(KVH, GROUP * HD, tok_rows)
    inner = jnp.sum(
        (attended * d_heads.astype(jnp.float32)).reshape(KVH, GROUP, HD, tok_rows), axis=2
    )
    d_queries, d_kv_hops = attention_backward(
        info, starts_row, queries, kv_stack, d_heads, lse, inner
    )
    received = d_kv_hops[0].astype(jnp.float32)
    for hop in range(1, hop_count + 1):
        received = received + from_behind(d_kv_hops[hop], "fsdp", -hop).astype(jnp.float32)
    d_query_raw = unrotate(d_queries.reshape(QH, HD, tok_rows) * score_scale, cosine, sine)
    d_key_raw = unrotate(received[:, :HD], cosine, sine)
    d_projected = jnp.concatenate(
        [
            d_query_raw.reshape(q_width, tok_rows),
            d_key_raw.reshape(kv_width, tok_rows),
            received[:, HD:].reshape(kv_width, tok_rows),
        ],
        axis=0,
    ).astype(jnp.bfloat16)
    grad_proj = dot(d_projected, normed, (1, 0))
    attn_terms = jnp.concatenate([grad_proj, grad_out], axis=0)
    attn_grad = scattered_sum(attn_terms).T
    d_normed = dot(d_projected, attn_full[:, :both], (0, 1))
    _, norm_one_back = jax.vjp(rms_norm, inputs, norm_gains[0])
    d_in_norm, d_gain_one = norm_one_back(d_normed)
    input_grad = d_middle + d_in_norm
    gain_grad = lax.psum(jnp.stack([d_gain_one, d_gain_two]), "fsdp")
    return (activations, input_grad, attn_grad, ffn_grad, gain_grad)


def solution(mesh):
    in_specs = (P("fsdp", None), P(None, "fsdp"), P(None, None, "fsdp"), P(), P(), P("fsdp", None))
    out_specs = (P("fsdp", None), P("fsdp", None), P(None, "fsdp"), P(None, None, "fsdp"), P())
    return jax.shard_map(
        on_device, mesh=mesh, in_specs=in_specs, out_specs=out_specs, check_vma=False
    )
```

time: 1600 us -> 1010 us (0.63); the launches traced: 1590 us -> 1030 us
  matrix products: 685 us -> 78 us
  waiting for transfers between devices: 313 us -> 570 us
  other arithmetic: 238 us -> 21.6 us
  local copies, waits for them, and re-layouts: 125 us -> 28.6 us
  starting transfers between devices: 64.3 us -> 141 us
  Pallas kernels: 0 us -> 66.2 us
  blocking collectives: 128 us -> 105 us
  loops' own time: 21.4 us -> 0 us
    dot_general x330 -> x15, matrix products: 685 us -> 78 us  [dot(): lax.dot_general(left, right, (((contract[0],), (contract[1],)), ((), ()))...]
    reduce_scatter x0 -> x3, waiting for transfers between devices: none -> 195 us  [scattered_sum(): lax.psum_scatter(terms.astype(jnp.bfloat16), 'fsdp', scatter_dimension=0,...]
    convert_element_type x7 -> x2, other arithmetic: 120 us -> 0.13 us  [the longest x1 0.13 us: on_device(): mixed = attended.reshape(q_width, tok_rows).astype(jnp.bfloat16)]
    ppermute x16, starting transfers between devices: 64.2 us -> 140 us  [from_behind(): lax.ppermute(value, axis, [(source, source + steps) for source in range(l...]
    pallas_call x0 -> x2, Pallas kernels: none -> 66.2 us  [the longest x1 37.4 us: attention_backward(): pl.pallas_call(backward_kernel, grid_spec=pltpu.PrefetchScalarGridSpec(nu...]
    unnamed x6 -> x7, waiting for transfers between devices: 91.6 us -> 140 us
    another operation x2 -> x1, local copies, waits for them, and re-layouts: 44.7 us -> 0.04 us  [on_device(): jnp.stack([own_block] + [from_behind(own_block, 'fsdp', hop) for hop in r...]
    while x620 -> x0, local copies, waits for them, and re-layouts: 36.9 us -> none
  transfers between devices with their start and end apart: 20 -> 22, of which waited for: 8 -> 10; matrix products, arithmetic and copies ran while one was open for 57% -> 8% of each run, Pallas kernels for 0% -> 6%
where the time goes in v1:
time: 1010 us; the launch traced here: 1030 us
  waiting for transfers between devices  570 us (56%)
  starting transfers between devices  141 us (14%)
  blocking collectives  105 us (10%)
  matrix products  78 us (8%)
  Pallas kernels  66.2 us (7%)
  local copies, waits for them, and re-layouts  28.6 us (3%)
  other arithmetic  21.6 us (2%)
  between operations  15.2 us (2%)
    reduce_scatter x3, waiting for transfers between devices, scattered_sum(): lax.psum_scatter(terms.astype(jnp.bfloat16), 'fsdp', scatter_dimension=0,...  195 us
    ppermute x16, waiting for transfers between devices, from_behind(): lax.ppermute(value, axis, [(source, source + steps) for source in range(l...  171 us
    unnamed x7, waiting for transfers between devices  140 us
    ppermute x16, starting transfers between devices, from_behind(): lax.ppermute(value, axis, [(source, source + steps) for source in range(l...  140 us
    psum x1, blocking collectives, on_device(): gain_grad = lax.psum(jnp.stack([d_gain_one, d_gain_two]), 'fsdp')  105 us
    dot_general x15, matrix products, dot(): lax.dot_general(left, right, (((contract[0],), (contract[1],)), ((), ()))...  78 us
    all_gather x1, waiting for transfers between devices, on_device(): attn_full = lax.all_gather(attn_weight, 'fsdp', axis=1, tiled=True)  63.4 us
    pallas_call x1, Pallas kernels, attention_backward(): pl.pallas_call(backward_kernel, grid_spec=pltpu.PrefetchScalarGridSpec(nu...  37.4 us
  transfers between devices with their start and end apart: 22, of which 10 were waited for; matrix products, arithmetic and copies ran while one was open for 8% of the time, Pallas kernels for 6%

profile of v1, /device:TPU:0, one launch (start us, length us, event | category | flops | bytes accessed | tf_op | source)
XLA Modules:
  0.0 1025.6 jit_solution(5068838075136002871)
XLA Ops:
  15.5 63.4 %all-gather.3.cloned.1.call-done = bf16[960,2560]{0,1:T(8,128)(2,1)} async-done(((bf16[960,80]{0,1:T(8,128)(2,1)}), bf16[960,2560]{0,1:T(8,128)(2,1)}) %all-gather.3.cloned.1.call-update) | async-done | bytes 4915216 | tf_op jit(solution)/shard_map/all_gather | solution.py:246
  78.9 4.2 convolution_bitcast_fusion
  84.9 4.1 collective-permute-start.7
  89.1 3.0 collective-permute-start.6
  94.9 3.5 collective-permute-start.1
  101.7 27.8 %collective-permute-start.3 = (bf16[640,512]{1,0:T(8,128)(2,1)S(1)}, bf16[640,512]{1,0:T(8,128)(2,1)S(1)}, u32[]{:S(2)}, u32[]{:S(2)}) collective-permute-start(bf16[640,512]{1,0:T(8,128)(2,1)S(1)} %pad_maximum_fusion.5), channel_id=1, source_target_pairs={{0,4},{1,5},{2,6},{3,7},{4,8},{5,9},{6,10},{7,11},{8,12},{9,13},{1... | collective-permute-start | bytes 1966088 | tf_op jit(solution)/shard_map/ppermute | solution.py:20
  132.0 84.4 %collective-permute-start.5 = (bf16[640,512]{1,0:T(8,128)(2,1)S(1)}, bf16[640,512]{1,0:T(8,128)(2,1)S(1)}, u32[]{:S(2)}, u32[]{:S(2)}) collective-permute-start(bf16[640,512]{1,0:T(8,128)(2,1)S(1)} %pad_maximum_fusion.5), channel_id=1, source_target_pairs={{0,6},{1,7},{2,8},{3,9},{4,10},{5,11},{6,12},{7,13},{8,14},{9,15},... | collective-permute-start | bytes 1966088 | tf_op jit(solution)/shard_map/ppermute | solution.py:20
  216.5 10.7 %collective-permute-done.5 = bf16[640,512]{1,0:T(8,128)(2,1)S(1)} collective-permute-done((bf16[640,512]{1,0:T(8,128)(2,1)S(1)}, bf16[640,512]{1,0:T(8,128)(2,1)S(1)}, u32[]{:S(2)}, u32[]{:S(2)}) %collective-permute-start.5) | collective-permute-done | bytes 655392 | tf_op jit(solution)/shard_map/ppermute | solution.py:20
  229.9 28.8 %attention_forward.1 = (f32[5,192,512]{2,1,0:T(8,128)S(1)}, f32[5,3,512]{2,1,0:T(4,128)S(1)}) custom-call(s32[3]{0:T(128)S(1)} %pad_add_fusion.info_ref, s32[1,512]{1,0:T(1,128)S(1)} %bitcast.112, bf16[5,192,512]{2,1,0:T(8,128)(2,1)S(1)} %bitcast.110, bf16[9,640,512]{2,1,0:T(8,128)(2,1)} %copy-done.25, bf16[9,640,512]{2,1,0:T(8,128)(2,1)} %copy-done.25), custom_call_target="tpu_custom_call" | custom-call | flops 36238786560 | bytes 12582912 | tf_op jit(solution)/shard_map/attention_forward/pallas_call | solution.py:177
  265.6 7.4 fusion.7
  274.5 6.0 fusion.5
  280.5 9.3 multiply_convert_fusion
  291.3 4.8 convolution_convert_fusion.1
  296.6 7.2 convolution_convert_fusion.2
  304.0 6.2 fusion.4
  310.2 5.7 multiply_reduce_fusion
  321.2 7.3 convolution_convert_fusion
  329.7 37.4 %attention_backward.1 = (f32[5,192,512]{2,1,0:T(8,128)S(1)}, bf16[9,5,128,512]{3,2,1,0:T(8,128)(2,1)}) custom-call(s32[3]{0:T(128)S(1)} %pad_add_fusion.info_ref, s32[1,512]{1,0:T(1,128)S(1)} %bitcast.113, bf16[5,192,512]{2,1,0:T(8,128)(2,1)S(1)} %bitcast.111, bf16[9,640,512]{2,1,0:T(8,128)(2,1)} %copy-done.25, bf16[9,640,512]{2,1,0:T(8,128)(2,1)} %copy-done.25, ...), custom_call_target="tpu_custom_call" | custom-call | flops 90596966400 | bytes 25165824 | tf_op jit(solution)/shard_map/attention_backward/pallas_call | solution.py:203
  367.2 3.0 slice_bitcast_fusion.20
  377.1 16.9 %collective-permute-done.8 = bf16[5,128,512]{2,1,0:T(8,128)(2,1)S(1)} collective-permute-done((bf16[5,128,512]{2,1,0:T(8,128)(2,1)S(1)}, bf16[5,128,512]{2,1,0:T(8,128)(2,1)S(1)}, u32[]{:S(2)}, u32[]{:S(2)}) %collective-permute-start.8) | collective-permute-done | bytes 655392 | tf_op jit(solution)/shard_map/ppermute | solution.py:20
  395.3 120.8 %collective-permute-done.15 = bf16[5,128,512]{2,1,0:T(8,128)(2,1)S(1)} collective-permute-done((bf16[5,128,512]{2,1,0:T(8,128)(2,1)S(1)}, bf16[5,128,512]{2,1,0:T(8,128)(2,1)S(1)}, u32[]{:S(2)}, u32[]{:S(2)}) %collective-permute-start.15) | collective-permute-done | bytes 655392 | tf_op jit(solution)/shard_map/ppermute | solution.py:20
  520.4 16.6 %collective-permute-done.10 = bf16[5,128,512]{2,1,0:T(8,128)(2,1)S(1)} collective-permute-done((bf16[5,128,512]{2,1,0:T(8,128)(2,1)S(1)}, bf16[5,128,512]{2,1,0:T(8,128)(2,1)S(1)}, u32[]{:S(2)}, u32[]{:S(2)}) %collective-permute-start.10) | collective-permute-done | bytes 655392 | tf_op jit(solution)/shard_map/ppermute | solution.py:20
  537.0 5.2 collective-permute-done.9
  546.3 3.6 pad_maximum_fusion
  549.9 7.9 copy.14
  559.3 7.1 add_convert_fusion
  566.4 5.5 fusion.16
  572.0 105.4 %psum.7 = f32[2,960]{1,0:T(2,128)} all-reduce(f32[2,960]{1,0:T(2,128)S(1)} %pad_maximum_fusion.7), channel_id=1, replica_groups=mesh['fsdp'=32] {'fsdp'}, use_global_device_ids=true, to_apply=%region_14.15 | all-reduce | flops 1920 | bytes 15360 | tf_op jit(solution)/shard_map/psum | solution.py:317
  677.4 3.3 fusion.18
  680.7 54.1 %reduce-scatter.7.cloned.1.call-done = bf16[80,960]{1,0:T(8,128)(2,1)} async-done(((bf16[2560,960]{1,0:T(8,128)(2,1)}), bf16[80,960]{1,0:T(8,128)(2,1)}) %reduce-scatter.7.cloned.1.call-update) | async-done | bytes 153616 | tf_op jit(solution)/shard_map/reduce_scatter | solution.py:224
  734.9 140.7 %reduce-scatter.11.cloned.1.call-done = bf16[80,960]{1,0:T(8,128)(2,1)} async-done(((bf16[2560,960]{1,0:T(8,128)(2,1)}), bf16[80,960]{1,0:T(8,128)(2,1)}) %reduce-scatter.11.cloned.1.call-update) | async-done | bytes 153616 | tf_op jit(solution)/shard_map/reduce_scatter | solution.py:224
  877.7 138.8 %reduce-scatter.13.cloned.1.call-done = bf16[80,960]{1,0:T(8,128)(2,1)} async-done(((bf16[2560,960]{1,0:T(8,128)(2,1)}), bf16[80,960]{1,0:T(8,128)(2,1)}) %reduce-scatter.13.cloned.1.call-update) | async-done | bytes 153616
  (167 shorter events, 60.2 us)
Async XLA Ops:
  7.2 71.7 %all-gather.3.cloned.1.call-start = ((), (), s32[]{:S(2)}) async-start(), calls=%async_computation.4 | async-start | bytes 5406720 | tf_op jit(solution)/shard_map/all_gather | solution.py:246
  7.9 256.8 %all-gather.5.cloned.1.call-start = ((), (), s32[]{:S(2)}) async-start(), calls=%async_computation.5 | async-start | bytes 16220160 | tf_op jit(solution)/shard_map/all_gather | solution.py:247
  8.6 672.1 %reduce-scatter.9.cloned.1.call-start = ((), (), s32[]{:S(2)}) async-start(), calls=%async_computation.7 | async-start | bytes 5406720 | tf_op jit(solution)/shard_map/reduce_scatter | solution.py:224
  14.3 68.7 %copy-start.30 = (f32[512]{0:T(512)}, f32[512]{0:T(512)S(1)}, u32[]{:S(2)}) copy-start(f32[512]{0:T(512)S(1)} %fusion.42) | copy-start | bytes 6148
  15.4 84.6 %copy-start.12 = (f32[32,512]{1,0:T(8,128)}, f32[32,512]{1,0:T(8,128)S(1)}, u32[]{:S(2)}) copy-start(f32[32,512]{1,0:T(8,128)S(1)} %get-tuple-element.53) | copy-start | bytes 196612
  15.5 84.6 %copy-start.14 = (f32[32,512]{1,0:T(8,128)}, f32[32,512]{1,0:T(8,128)S(1)}, u32[]{:S(2)}) copy-start(f32[32,512]{1,0:T(8,128)S(1)} %get-tuple-element.54) | copy-start | bytes 196612
  84.9 142.4 %collective-permute-start.7 = (bf16[640,512]{1,0:T(8,128)(2,1)S(1)}, bf16[640,512]{1,0:T(8,128)(2,1)S(1)}, u32[]{:S(2)}, u32[]{:S(2)}) collective-permute-start(bf16[640,512]{1,0:T(8,128)(2,1)S(1)} %pad_maximum_fusion.5), channel_id=1, source_target_pairs={{0,8},{1,9},{2,10},{3,11},{4,12},{5,13},{6,14},{7,15},{8,16},{9,17... | collective-permute-start | bytes 1966088 | tf_op jit(solution)/shard_map/ppermute | solution.py:20
  89.1 138.2 %collective-permute-start.6 = (bf16[640,512]{1,0:T(8,128)(2,1)S(1)}, bf16[640,512]{1,0:T(8,128)(2,1)S(1)}, u32[]{:S(2)}, u32[]{:S(2)}) collective-permute-start(bf16[640,512]{1,0:T(8,128)(2,1)S(1)} %pad_maximum_fusion.5), channel_id=1, source_target_pairs={{0,7},{1,8},{2,9},{3,10},{4,11},{5,12},{6,13},{7,14},{8,15},{9,16}... | collective-permute-start | bytes 1966088 | tf_op jit(solution)/shard_map/ppermute | solution.py:20
  92.1 39.9 %collective-permute-start.2 = (bf16[640,512]{1,0:T(8,128)(2,1)S(1)}, bf16[640,512]{1,0:T(8,128)(2,1)S(1)}, u32[]{:S(2)}, u32[]{:S(2)}) collective-permute-start(bf16[640,512]{1,0:T(8,128)(2,1)S(1)} %pad_maximum_fusion.5), channel_id=1, source_target_pairs={{0,3},{1,4},{2,5},{3,6},{4,7},{5,8},{6,9},{7,10},{8,11},{9,12},{10... | collective-permute-start | bytes 1966088 | tf_op jit(solution)/shard_map/ppermute | solution.py:20
  94.9 34.6 %collective-permute-start.1 = (bf16[640,512]{1,0:T(8,128)(2,1)S(1)}, bf16[640,512]{1,0:T(8,128)(2,1)S(1)}, u32[]{:S(2)}, u32[]{:S(2)}) collective-permute-start(bf16[640,512]{1,0:T(8,128)(2,1)S(1)} %pad_maximum_fusion.5), channel_id=1, source_target_pairs={{0,2},{1,3},{2,4},{3,5},{4,6},{5,7},{6,8},{7,9},{8,10},{9,11},{10,... | collective-permute-start | bytes 1966088 | tf_op jit(solution)/shard_map/ppermute | solution.py:20
  98.4 3.3 collective-permute-start
  100.7 126.8 %copy-start = (bf16[15,64,512]{2,1,0:T(8,128)(2,1)}, bf16[15,64,512]{2,1,0:T(8,128)(2,1)S(1)}, u32[]{:S(2)}) copy-start(bf16[15,64,512]{2,1,0:T(8,128)(2,1)S(1)} %maximum_multiply_fusion) | copy-start | bytes 2949124
  101.7 114.7 %collective-permute-start.3 = (bf16[640,512]{1,0:T(8,128)(2,1)S(1)}, bf16[640,512]{1,0:T(8,128)(2,1)S(1)}, u32[]{:S(2)}, u32[]{:S(2)}) collective-permute-start(bf16[640,512]{1,0:T(8,128)(2,1)S(1)} %pad_maximum_fusion.5), channel_id=1, source_target_pairs={{0,4},{1,5},{2,6},{3,7},{4,8},{5,9},{6,10},{7,11},{8,12},{9,13},{1... | collective-permute-start | bytes 1966088 | tf_op jit(solution)/shard_map/ppermute | solution.py:20
  129.6 86.9 %collective-permute-start.4 = (bf16[640,512]{1,0:T(8,128)(2,1)S(1)}, bf16[640,512]{1,0:T(8,128)(2,1)S(1)}, u32[]{:S(2)}, u32[]{:S(2)}) collective-permute-start(bf16[640,512]{1,0:T(8,128)(2,1)S(1)} %pad_maximum_fusion.5), channel_id=1, source_target_pairs={{0,5},{1,6},{2,7},{3,8},{4,9},{5,10},{6,11},{7,12},{8,13},{9,14},{... | collective-permute-start | bytes 1966088 | tf_op jit(solution)/shard_map/ppermute | solution.py:20
  132.0 95.3 %collective-permute-start.5 = (bf16[640,512]{1,0:T(8,128)(2,1)S(1)}, bf16[640,512]{1,0:T(8,128)(2,1)S(1)}, u32[]{:S(2)}, u32[]{:S(2)}) collective-permute-start(bf16[640,512]{1,0:T(8,128)(2,1)S(1)} %pad_maximum_fusion.5), channel_id=1, source_target_pairs={{0,6},{1,7},{2,8},{3,9},{4,10},{5,11},{6,12},{7,13},{8,14},{9,15},... | collective-permute-start | bytes 1966088 | tf_op jit(solution)/shard_map/ppermute | solution.py:20
  296.1 438.7 %reduce-scatter.7.cloned.1.call-start = ((), (), s32[]{:S(2)}) async-start(), calls=%async_computation.6 | async-start | bytes 5406720 | tf_op jit(solution)/shard_map/reduce_scatter | solution.py:224
  303.9 571.7 %reduce-scatter.11.cloned.1.call-start = ((), (), s32[]{:S(2)}) async-start(), calls=%async_computation.8 | async-start | bytes 5406720 | tf_op jit(solution)/shard_map/reduce_scatter | solution.py:224
  328.6 688.0 %reduce-scatter.13.cloned.1.call-start = ((), (), s32[]{:S(2)}) async-start(), calls=%async_computation.9 | async-start | bytes 5406720
  370.2 148.4 %copy-start.13 = (f32[32,512]{1,0:T(8,128)S(1)}, f32[32,512]{1,0:T(8,128)}, u32[]{:S(2)}) copy-start(f32[32,512]{1,0:T(8,128)} %copy-done.12) | copy-start | bytes 196612
  370.2 148.4 %copy-start.15 = (f32[32,512]{1,0:T(8,128)S(1)}, f32[32,512]{1,0:T(8,128)}, u32[]{:S(2)}) copy-start(f32[32,512]{1,0:T(8,128)} %copy-done.14) | copy-start | bytes 196612
  370.2 23.8 %collective-permute-start.8 = (bf16[5,128,512]{2,1,0:T(8,128)(2,1)S(1)}, bf16[5,128,512]{2,1,0:T(8,128)(2,1)S(1)}, u32[]{:S(2)}, u32[]{:S(2)}) collective-permute-start(bf16[5,128,512]{2,1,0:T(8,128)(2,1)S(1)} %get-tuple-element.35), channel_id=1, source_target_pairs={{1,0},{2,1},{3,2},{4,3},{5,4},{6,5},{7,6},{8,7},{9,8},{10,9},{11,1... | collective-permute-start | bytes 1966088 | tf_op jit(solution)/shard_map/ppermute | solution.py:20
  371.6 144.4 %collective-permute-start.15 = (bf16[5,128,512]{2,1,0:T(8,128)(2,1)S(1)}, bf16[5,128,512]{2,1,0:T(8,128)(2,1)S(1)}, u32[]{:S(2)}, u32[]{:S(2)}) collective-permute-start(bf16[5,128,512]{2,1,0:T(8,128)(2,1)S(1)} %get-tuple-element.36), channel_id=1, source_target_pairs={{8,0},{9,1},{10,2},{11,3},{12,4},{13,5},{14,6},{15,7},{16,8},{17,9... | collective-permute-start | bytes 1966088 | tf_op jit(solution)/shard_map/ppermute | solution.py:20
  372.9 144.4 %collective-permute-start.14 = (bf16[5,128,512]{2,1,0:T(8,128)(2,1)S(1)}, bf16[5,128,512]{2,1,0:T(8,128)(2,1)S(1)}, u32[]{:S(2)}, u32[]{:S(2)}) collective-permute-start(bf16[5,128,512]{2,1,0:T(8,128)(2,1)S(1)} %get-tuple-element.37), channel_id=1, source_target_pairs={{7,0},{8,1},{9,2},{10,3},{11,4},{12,5},{13,6},{14,7},{15,8},{16,9}... | collective-permute-start | bytes 1966088 | tf_op jit(solution)/shard_map/ppermute | solution.py:20
  374.2 146.1 %collective-permute-start.13 = (bf16[5,128,512]{2,1,0:T(8,128)(2,1)S(1)}, bf16[5,128,512]{2,1,0:T(8,128)(2,1)S(1)}, u32[]{:S(2)}, u32[]{:S(2)}) collective-permute-start(bf16[5,128,512]{2,1,0:T(8,128)(2,1)S(1)} %get-tuple-element.38), channel_id=1, source_target_pairs={{6,0},{7,1},{8,2},{9,3},{10,4},{11,5},{12,6},{13,7},{14,8},{15,9},... | collective-permute-start | bytes 1966088 | tf_op jit(solution)/shard_map/ppermute | solution.py:20
  375.5 144.8 %collective-permute-start.12 = (bf16[5,128,512]{2,1,0:T(8,128)(2,1)S(1)}, bf16[5,128,512]{2,1,0:T(8,128)(2,1)S(1)}, u32[]{:S(2)}, u32[]{:S(2)}) collective-permute-start(bf16[5,128,512]{2,1,0:T(8,128)(2,1)S(1)} %get-tuple-element.39), channel_id=1, source_target_pairs={{5,0},{6,1},{7,2},{8,3},{9,4},{10,5},{11,6},{12,7},{13,8},{14,9},{... | collective-permute-start | bytes 1966088 | tf_op jit(solution)/shard_map/ppermute | solution.py:20
  377.1 142.0 %copy-start.8 = (f32[512,960]{0,1:T(8,128)S(1)}, f32[512,960]{0,1:T(8,128)}, u32[]{:S(2)}) copy-start(f32[512,960]{0,1:T(8,128)} %copy-done.7) | copy-start | bytes 5898244
  377.1 142.0 %copy-start.18 = (bf16[5,192,512]{2,1,0:T(8,128)(2,1)S(1)}, bf16[5,192,512]{2,1,0:T(8,128)(2,1)}, u32[]{:S(2)}) copy-start(bf16[5,192,512]{2,1,0:T(8,128)(2,1)} %copy-done.17) | copy-start | bytes 2949124
  394.0 126.4 %collective-permute-start.11 = (bf16[5,128,512]{2,1,0:T(8,128)(2,1)S(1)}, bf16[5,128,512]{2,1,0:T(8,128)(2,1)S(1)}, u32[]{:S(2)}, u32[]{:S(2)}) collective-permute-start(bf16[5,128,512]{2,1,0:T(8,128)(2,1)S(1)} %get-tuple-element.40), channel_id=1, source_target_pairs={{4,0},{5,1},{6,2},{7,3},{8,4},{9,5},{10,6},{11,7},{12,8},{13,9},{1... | collective-permute-start | bytes 1966088 | tf_op jit(solution)/shard_map/ppermute | solution.py:20
  516.0 21.0 %collective-permute-start.10 = (bf16[5,128,512]{2,1,0:T(8,128)(2,1)S(1)}, bf16[5,128,512]{2,1,0:T(8,128)(2,1)S(1)}, u32[]{:S(2)}, u32[]{:S(2)}) collective-permute-start(bf16[5,128,512]{2,1,0:T(8,128)(2,1)S(1)} %get-tuple-element.41), channel_id=1, source_target_pairs={{3,0},{4,1},{5,2},{6,3},{7,4},{8,5},{9,6},{10,7},{11,8},{12,9},{13... | collective-permute-start | bytes 1966088 | tf_op jit(solution)/shard_map/ppermute | solution.py:20
  517.3 24.8 %collective-permute-start.9 = (bf16[5,128,512]{2,1,0:T(8,128)(2,1)S(1)}, bf16[5,128,512]{2,1,0:T(8,128)(2,1)S(1)}, u32[]{:S(2)}, u32[]{:S(2)}) collective-permute-start(bf16[5,128,512]{2,1,0:T(8,128)(2,1)S(1)} %get-tuple-element.42), channel_id=1, source_target_pairs={{2,0},{3,1},{4,2},{5,3},{6,4},{7,5},{8,6},{9,7},{10,8},{11,9},{12,... | collective-permute-start | bytes 1966088 | tf_op jit(solution)/shard_map/ppermute | solution.py:20
  566.4 111.0 %copy-start.27 = (f32[512]{0:T(512)S(1)}, f32[512]{0:T(512)}, u32[]{:S(2)}) copy-start(f32[512]{0:T(512)} %copy-done.26) | copy-start | bytes 6148
  566.4 111.0 %copy-start.9 = (f32[512,960]{0,1:T(8,128)S(1)}, f32[512,960]{0,1:T(8,128)}, u32[]{:S(2)}) copy-start(f32[512,960]{0,1:T(8,128)} %copy-done.7) | copy-start | bytes 5898244
  (28 other events, 286.9 us)
Sparse Core Ops, SparseCore 0:
  10.9 67.9 all-gather.2
  81.7 154.8 all-gather.4
  296.3 294.6 reduce-scatter.8
  593.1 141.7 reduce-scatter.6
  737.0 138.5 reduce-scatter.10
  877.7 138.7 reduce-scatter.12
